TPU v7x, 512 devices: a whole 4x8x8 slice. The times are simulated.
512 devices in a mesh: dp: 8 (over z), fsdp: 16 (over y, x_lo), tensor: 4 (over x_hi, core).
Axes of the slice: x: 4 (x_hi: 2, x_lo: 2; x = x_hi * 2 + x_lo), y: 8, z: 8, core: 2. Of those that a mesh axis runs over, the one named last changes fastest.
Arguments:
- query: bfloat16 [8, 2048, 3072], P('dp', 'fsdp', 'tensor'), may hold values from -120 to 120
- key_in: bfloat16 [8, 2048, 3072], P('dp', 'fsdp', 'tensor'), may hold values from -9 to 9
- value: bfloat16 [8, 2048, 3072], P('dp', 'fsdp', 'tensor'), may hold values from -6 to 6
- segment_ids: int32 [8, 2048], P('dp'), may hold values from 0 to 7, never falling along the last dimension, each value on 1 to 1024 neighbouring positions
- blend: float32 [1], replicated, may hold values from 0.1 to 0.9
- w_first: bfloat16 [6144, 3072], P(('dp', 'fsdp'), 'tensor'), may hold values from -0.109375 to 0.109375
- w_second: bfloat16 [6144, 3072], P(('dp', 'fsdp'), 'tensor'), may hold values from -0.109375 to 0.109375
Outputs:
- mixed: bfloat16 [8, 2048, 6144], P('dp', 'fsdp', 'tensor')
Inputs may be any that keep to these rules, and one draw needn't show every extreme that they name: `segment_ids`: within each pack image numbers never fall, each of the 8 images holds 1 to 1024 patches, and one holds exactly 1024.
All inputs are finite; a program needn't handle non-finite values.
Results may differ from a plain program's by a relative error of at most 0.012.
Values may be sent and summed in bfloat16 or wider, within the bound.
A program may use at most 64 MiB of HBM per device.

v0:
```python
import jax
import jax.numpy as jnp
from jax import lax
from jax.sharding import PartitionSpec as P

HEAD_DIM = 128


def per_device(query, key_in, value, segment_ids, blend, w_first, w_second):
    rows = query.shape[1]
    width_local = query.shape[2]
    heads_local = width_local // HEAD_DIM
    keys_all, values_all = (
        lax.all_gather(key_in, "fsdp", axis=1, tiled=True),
        lax.all_gather(value, "fsdp", axis=1, tiled=True),
    )
    seg_all = segment_ids[0]
    begin = lax.axis_index("fsdp") * rows
    seg_rows = lax.dynamic_slice_in_dim(seg_all, begin, rows, 0)
    same = seg_rows[:, None] == seg_all[None, :]
    queries = query[0].reshape(rows, heads_local, HEAD_DIM)
    keyed = keys_all[0].reshape(-1, heads_local, HEAD_DIM)
    valued = values_all[0].reshape(-1, heads_local, HEAD_DIM)
    scores = jnp.einsum(
        "qhd,khd->hqk", queries, keyed, preferred_element_type=jnp.float32
    ) * HEAD_DIM ** (-0.5)
    scores = jnp.where(same[None, :, :], scores, jnp.float32(-1e30))
    top = jnp.max(scores, axis=2, keepdims=True)
    expo = jnp.exp(scores - top)
    probs = (expo / jnp.sum(expo, axis=2, keepdims=True)).astype(jnp.bfloat16)
    attended = jnp.einsum("hqk,khd->qhd", probs, valued, preferred_element_type=jnp.float32)
    attended = attended.astype(jnp.bfloat16).reshape(rows, width_local)
    coef = blend[0]
    blended = (
        (1.0 - coef) * w_first.astype(jnp.float32) + coef * w_second.astype(jnp.float32)
    ).astype(jnp.bfloat16)
    dims = (((1,), (1,)), ((), ()))
    partial_value = lax.dot_general(
        attended,
        lax.all_gather(blended, ("dp", "fsdp"), axis=0, tiled=True),
        dims,
        preferred_element_type=jnp.float32,
    ).astype(jnp.bfloat16)
    summed = lax.psum_scatter(
        partial_value.astype(jnp.float32).astype(jnp.bfloat16),
        "tensor",
        scatter_dimension=1,
        tiled=True,
    ).astype(jnp.float32)
    return summed.astype(jnp.bfloat16).reshape(1, rows, summed.shape[1])


def solution(mesh):
    in_specs = (
        P("dp", "fsdp", "tensor"),
        P("dp", "fsdp", "tensor"),
        P("dp", "fsdp", "tensor"),
        P("dp", None),
        P(),
        P(("dp", "fsdp"), "tensor"),
        P(("dp", "fsdp"), "tensor"),
    )
    out_specs = P("dp", "fsdp", "tensor")
    return jax.shard_map(
        per_device, mesh=mesh, in_specs=in_specs, out_specs=out_specs, check_vma=False
    )
```

profile of v0, /device:TPU:1, one launch (start us, length us, event | category | flops | bytes accessed | tf_op | source)
XLA Modules:
  0.0 864.2 jit_solution(3240280498170873673)
XLA Ops:
  6.5 0.0 all-gather.6.cloned.1.call-start
  6.5 0.7 all-gather.6.cloned.1.call-update
  7.3 0.0 all-gather.4.cloned.1.call-start
  7.3 1.7 copy.11
  9.0 0.0 all-gather.4.cloned.1.call-update
  9.1 0.0 all-gather.8.cloned.1.call-start
  9.8 1.6 add_convert_fusion
  11.3 0.0 all-gather.8.cloned.1.call-update
  11.4 0.0 reduce-scatter.2.cloned.1.call-start
  11.4 1.7 copy.10
  13.2 0.7 dynamic-slice_bitcast_fusion
  13.8 0.9 broadcast_compare_fusion
  14.7 80.6 %all-gather.6.cloned.1.call-done = bf16[1,2048,768]{2,1,0:T(8,128)(2,1)} async-done(((bf16[1,128,768]{2,1,0:T(8,128)(2,1)}), bf16[1,2048,768]{2,1,0:T(8,128)(2,1)}) %all-gather.6.cloned.1.call-update) | async-done | bytes 3145744 | tf_op jit(solution)/shard_map/all_gather | solution.py:15
  95.3 3.2 copy.14
  98.5 93.6 %all-gather.4.cloned.1.call-done = bf16[1,2048,768]{1,2,0:T(8,128)(2,1)} async-done(((bf16[1,128,768]{1,2,0:T(8,128)(2,1)}), bf16[1,2048,768]{1,2,0:T(8,128)(2,1)}) %all-gather.4.cloned.1.call-update) | async-done | bytes 3145744 | tf_op jit(solution)/shard_map/all_gather | solution.py:14
  192.1 7.1 fusion.11
  199.1 3.9 fusion.6
  203.0 520.2 %all-gather.8.cloned.1.call-done = bf16[6144,768]{1,0:T(8,128)(2,1)} async-done(((bf16[48,768]{1,0:T(8,128)(2,1)}), bf16[6144,768]{1,0:T(8,128)(2,1)}) %all-gather.8.cloned.1.call-update) | async-done | bytes 9437200 | tf_op jit(solution)/shard_map/all_gather | solution.py:40
  723.2 8.0 convolution_convert_fusion
  731.2 0.0 reduce-scatter.2.cloned.1.call-update
  731.2 126.4 %reduce-scatter.2.cloned.1.call-done = bf16[128,1536]{1,0:T(8,128)(2,1)} async-done(((bf16[128,6144]{1,0:T(8,128)(2,1)}), bf16[128,1536]{1,0:T(8,128)(2,1)}) %reduce-scatter.2.cloned.1.call-update) | async-done | bytes 393232 | tf_op jit(solution)/shard_map/reduce_scatter | solution.py:44
Async XLA Ops:
  6.5 88.8 %all-gather.6.cloned.1.call-start = ((), (), s32[]{:S(2)}) async-start(), calls=%async_computation.2 | async-start | bytes 3342336 | tf_op jit(solution)/shard_map/all_gather | solution.py:15
  7.3 184.8 %all-gather.4.cloned.1.call-start = ((), (), s32[]{:S(2)}) async-start(), calls=%async_computation.1 | async-start | bytes 3342336 | tf_op jit(solution)/shard_map/all_gather | solution.py:14
  9.1 714.1 %all-gather.8.cloned.1.call-start = ((), (), s32[]{:S(2)}) async-start(), calls=%async_computation.3 | async-start | bytes 9510912 | tf_op jit(solution)/shard_map/all_gather | solution.py:40
  11.4 846.3 %reduce-scatter.2.cloned.1.call-start = ((), (), s32[]{:S(2)}) async-start(), calls=%async_computation.4 | async-start | bytes 1966080 | tf_op jit(solution)/shard_map/reduce_scatter | solution.py:44
Sparse Core Ops, SparseCore 0:
  9.4 85.8 all-gather.5
  97.3 94.7 all-gather.3
  194.2 528.9 all-gather.7
  731.4 126.2 reduce-scatter.1
where the time goes:
time: 865 us; the launch traced here: 864 us
  waiting for transfers between devices  822 us (95%)
  matrix products  19 us (2%)
  between operations  13.8 us (2%)
    all_gather x1, waiting for transfers between devices, per_device(): lax.all_gather(blended, ('dp', 'fsdp'), axis=0, tiled=True)  520 us
    reduce_scatter x1, waiting for transfers between devices, per_device(): lax.psum_scatter(partial_value.astype(jnp.float32).astype(jnp.bfloat16),...  126 us
    all_gather x1, waiting for transfers between devices, per_device(): lax.all_gather(key_in, 'fsdp', axis=1, tiled=True)  93.6 us
    all_gather x1, waiting for transfers between devices, per_device(): lax.all_gather(value, 'fsdp', axis=1, tiled=True)  80.6 us
  transfers between devices with their start and end apart: 4, of which 4 were waited for; matrix products, arithmetic and copies ran while one was open for 2% of the time, Pallas kernels for 0%

commit v1 on v0

v1 whole, which is shorter than its diff:
```python
import functools
import heapq

import jax
import jax.numpy as jnp
from jax import lax
from jax.experimental import pallas as pl
from jax.experimental.pallas import tpu as pltpu
from jax.sharding import PartitionSpec as P

HEAD_DIM = 128
MESH = pl.DeviceIdType.MESH
NT = (((1,), (1,)), ((), ()))


class Node:
    def __init__(self, name, deps, cost, link=None, rank=0):
        self.name, self.deps, self.cost, self.link, self.rank = name, list(deps), cost, link, rank


def order_of(nodes, latency=1.5):
    by_name = {node.name: node for node in nodes}
    position = {node.name: i for i, node in enumerate(nodes)}
    feeds = {node.name: False for node in nodes}
    for node in nodes:
        if node.link is not None:
            for dep in node.deps:
                feeds[dep] = True
    done, started, waited = set(), set(), set()
    arrivals, free, order, now = [], {}, [], 0.0
    while len(done) < len(nodes):
        for node in nodes:
            if node.link is not None and node.name not in started and all(d in done for d in node.deps):
                for d in node.deps:
                    if by_name[d].link is not None and d not in waited:
                        waited.add(d)
                        order.append(("wait", d))
                started.add(node.name)
                order.append(("start", node.name))
                begin = max(now, free.get(node.link, 0.0))
                free[node.link] = begin + node.cost
                heapq.heappush(arrivals, (begin + node.cost + latency, position[node.name], node.name))
        if arrivals and arrivals[0][0] <= now:
            name = heapq.heappop(arrivals)[2]
            done.add(name)
            if feeds[name] and name not in waited:
                waited.add(name)
                order.append(("wait", name))
            continue
        ready = [n for n in nodes if n.link is None and n.name not in done and all(d in done for d in n.deps)]
        if ready:
            node = min(ready, key=lambda n: (n.rank, position[n.name]))
            for d in node.deps:
                if by_name[d].link is not None and d not in waited:
                    waited.add(d)
                    order.append(("wait", d))
            order.append(("compute", node.name))
            now += node.cost
            done.add(node.name)
            continue
        now = max(now, arrivals[0][0])
    return order


def plan(n_y, n_z, heads):
    nodes = []

    def add(name, deps, cost, link=None, rank=0):
        nodes.append(Node(name, deps, cost, link, rank))
        return name

    w_cost, kv_cost = 1.5, 2.0
    offsets = [0]
    for k in range(1, n_y // 2 + 1):
        offsets += [-k, k] if 2 * k < n_y else [-k]
    add(("blend",), [], 0.3, rank=-3)
    for j in offsets:
        if j == 0:
            continue
        link = "y+" if j < 0 else "y-"
        sign = 1 if j > 0 else -1
        add(("wy", j), [("wy", j - sign)] if abs(j) > 1 else [("blend",)], w_cost, link)
    for slot, j in enumerate(offsets):
        source = ("wy", j) if j else ("blend",)
        up = n_z // 2 - (slot % 2)
        for k in range(1, n_z // 2 + 1):
            for way, most in ((1, up), (-1, n_z - 1 - up)):
                if k <= most:
                    link = "z+" if way > 0 else "z-"
                    add(("wz", slot, way * k), [("wz", slot, way * (k - 1))] if k > 1 else [source], w_cost, link)
    add(("local",), [], 0.5, rank=-2)
    for part in ("k", "v", "q"):
        add(("x", part), [], kv_cost, "x")
    for part, up in (("k", n_y // 2), ("v", n_y - 1 - n_y // 2)):
        for own in (1, 0):
            source = ("local",) if own else ("x", part)
            for k in range(1, n_y // 2 + 1):
                for way, most in ((1, up), (-1, n_y - 1 - up)):
                    if k <= most:
                        link = "y+" if way > 0 else "y-"
                        add((part, own, way * k), [(part, own, way * (k - 1))] if k > 1 else [source], kv_cost, link)
    add(("mask",), [], 1.0, rank=-1)
    held = [("mask",), ("local",)] + [n.name for n in nodes if n.name[0] in ("k", "v", "x")]
    for h in range(heads):
        for half in range(2):
            add(("attn", h, half), held, 0.8)
        add(("a", h), [("attn", h, 0), ("attn", h, 1)], 1.3, "x")
    ready = [("a", h) for h in range(heads)]
    for slot, j in enumerate(offsets):
        shards = [n.name for n in nodes if n.name[0] == "wz" and n.name[1] == slot]
        source = ("wy", j) if j else ("blend",)
        add(("proj", slot), ready + shards + [source], 0.4, rank=slot)
        add(("c", slot), [("proj", slot)], 0.3, "core")
        add(("add", slot), [("c", slot)], 0.1, rank=slot - 20)
        for r in range(3):
            add(("e", slot, r), [("add", slot)], 0.5 if r else 1.0, "x")
        add(("sum", slot), [("e", slot, r) for r in range(3)], 0.1, rank=slot + 20)
    add(("last",), [("sum", slot) for slot in range(n_y)], 0.5, rank=100)
    return nodes, offsets


def kernel(
    n_y, n_z, order, ids, offsets,
    q_hbm, k_hbm, v_hbm, seg_ref, blend_ref, w_first, w_second, out_ref,
    kbuf, vbuf, qbuf, bias, wbuf, attbuf, p_own, p_send, c_recv, s_send, s_keep, e_recv, out_t,
    local_sem, send_sem, recv_sem,
):
    z = lax.axis_index("dp")
    f = lax.axis_index("fsdp")
    t = lax.axis_index("tensor")
    y, x = f // 2, f % 2
    x_hi, core = t // 2, t % 2
    rows = q_hbm.shape[1]
    half_width = kbuf.shape[1]
    heads = half_width // HEAD_DIM
    piece = w_first.shape[0]
    x_other = f + 1 - 2 * x
    t_core = t + 1 - 2 * core
    t_hi = t + 2 - 4 * x_hi

    def y_at(d):
        return (y + d + 2 * n_y) % n_y

    def z_at(d):
        return (z + d + 2 * n_z) % n_z

    def to(dp=None, fsdp=None, tensor=None):
        return (z if dp is None else dp, f if fsdp is None else fsdp, t if tensor is None else tensor)

    partners = [
        to(fsdp=x_other),
        to(tensor=t_core),
        to(tensor=t_hi),
        to(fsdp=x_other, tensor=t_hi),
        to(fsdp=y_at(1) * 2 + x),
        to(fsdp=y_at(-1) * 2 + x),
        to(dp=z_at(1)),
        to(dp=z_at(-1)),
    ]

    mine = pl.ds(pl.multiple_of(x * half_width, HEAD_DIM), half_width)
    theirs = pl.ds(pl.multiple_of((1 - x) * half_width, HEAD_DIM), half_width)

    def token_rows(y_index, x_index):
        return pl.ds(pl.multiple_of((y_index * 2 + x_index) * rows, rows), rows)

    bufs = {"k": kbuf, "v": vbuf, "q": qbuf}
    hbm = {"k": k_hbm, "v": v_hbm, "q": q_hbm}

    def q_rows(x_index):
        return pl.ds(pl.multiple_of(x_index * rows, rows), rows)

    locals_ = []
    for i, part in enumerate(("k", "v", "q")):
        at = q_rows(x) if part == "q" else token_rows(y, x)
        locals_.append(pltpu.make_async_copy(hbm[part].at[0, :, mine], bufs[part].at[at], local_sem.at[i]))
    for copy in locals_:
        copy.start()

    barrier = pltpu.get_barrier_semaphore()
    for partner in partners:
        pl.semaphore_signal(barrier, inc=1, device_id=partner, device_id_type=MESH)
    pl.semaphore_wait(barrier, len(partners))

    def copy_of(name, arriving):
        kind = name[0]
        if kind == "wy":
            j = name[1]
            sign = 1 if j > 0 else -1
            src = dst = wbuf.at[y_at(j if arriving else j - sign), z]
            who = to(fsdp=y_at(-sign) * 2 + x)
        elif kind == "wz":
            slot, k = name[1:]
            way = 1 if k > 0 else -1
            src = dst = wbuf.at[y_at(offsets[slot]), z_at(-k if arriving else -(k - way))]
            who = to(dp=z_at(way))
        elif kind == "x":
            part = name[1]
            from_x = 1 - x if arriving else x
            at = q_rows(from_x) if part == "q" else token_rows(y, from_x)
            dst = bufs[part].at[at]
            src = dst if arriving else hbm[part].at[0, :, theirs]
            who = to(fsdp=x_other)
        elif kind in ("k", "v"):
            own, k = name[1:]
            way = 1 if k > 0 else -1
            part_x = x if own else 1 - x
            src = dst = bufs[kind].at[token_rows(y_at(-k if arriving else -(k - way)), part_x)]
            who = to(fsdp=y_at(way) * 2 + x)
        elif kind == "a":
            h = name[1]
            src = dst = attbuf.at[((1 - x) if arriving else x) * heads + h]
            who = to(fsdp=x_other)
        elif kind == "c":
            slot = name[1]
            dst = c_recv.at[slot]
            src = dst if arriving else p_send.at[slot]
            who = to(tensor=t_core)
        else:
            slot, r = name[1:]
            dst = e_recv.at[r, slot]
            src = dst if arriving else s_send.at[r, slot]
            who = partners[(2, 3, 0)[r]]
        i = ids[name]
        return pltpu.make_async_remote_copy(
            src_ref=src, dst_ref=dst, send_sem=send_sem.at[i], recv_sem=recv_sem.at[i],
            device_id=who, device_id_type=MESH,
        )

    def blend():
        coef = blend_ref[0]
        mixed = (1.0 - coef) * w_first[...].astype(jnp.float32) + coef * w_second[...].astype(jnp.float32)
        wbuf[y, z] = mixed.astype(jnp.bfloat16)

    def mask():
        count = 2 * rows
        row = seg_ref[:, pl.ds(pl.multiple_of(y * count, count), count)].astype(jnp.float32)
        on = lax.broadcasted_iota(jnp.int32, (count, count), 0) == lax.broadcasted_iota(jnp.int32, (count, count), 1)
        column = jnp.sum(jnp.where(on, jnp.broadcast_to(row, (count, count)), 0.0), axis=1, keepdims=True)
        keys = seg_ref[...].astype(jnp.float32)
        bias[...] = jnp.where(column == keys, jnp.float32(0.0), jnp.float32(-1e30))

    def attn(h, half):
        at, cols = slice(half * rows, (half + 1) * rows), slice(h * HEAD_DIM, (h + 1) * HEAD_DIM)
        scores = lax.dot_general(qbuf[at, cols], kbuf[:, cols], NT, preferred_element_type=jnp.float32)
        scores = scores * HEAD_DIM ** (-0.5) + bias[at, :]
        top = jnp.max(scores, axis=1, keepdims=True)
        expo = jnp.exp(scores - top)
        total = jnp.sum(expo, axis=1, keepdims=True)
        result = jnp.dot(expo.astype(jnp.bfloat16), vbuf[:, cols], preferred_element_type=jnp.float32)
        attbuf[x * heads + h, at, :] = (result / total).astype(jnp.bfloat16)

    def proj(slot):
        attended = jnp.concatenate([attbuf[i] for i in range(2 * heads)], axis=1)
        shards = wbuf.at[y_at(offsets[slot])]
        per = n_z // 4
        for hi in range(2):
            for same in range(2):
                first = (hi * 2 + (core if same else 1 - core)) * per
                weight = shards[pl.ds(first, per)].reshape(per * piece, attended.shape[1])
                part = lax.dot_general(weight, attended, NT, preferred_element_type=jnp.float32).astype(jnp.bfloat16)
                (p_own if same else p_send)[slot, hi] = part

    def add(slot):
        for away in range(2):
            hi = (1 - x_hi) if away else x_hi
            both = (p_own[slot, hi].astype(jnp.float32) + c_recv[slot, hi].astype(jnp.float32)).astype(jnp.bfloat16)
            first, second = both[:, :rows], both[:, rows:]
            keep = jnp.where(x == 0, first, second)
            move = jnp.where(x == 0, second, first)
            if away:
                s_send[0, slot] = keep
                s_send[1, slot] = move
            else:
                s_keep[slot] = keep
                s_send[2, slot] = move

    def total(slot):
        at = y_at(offsets[slot])
        per = n_z // 4
        own = s_keep[slot].astype(jnp.float32) + e_recv[0, slot].astype(jnp.float32)
        other = e_recv[1, slot].astype(jnp.float32) + e_recv[2, slot].astype(jnp.float32)
        for i in range(per):
            part = slice(i * piece, (i + 1) * piece)
            out_t[i, at, x] = own[part].astype(jnp.bfloat16)
            out_t[i, at, 1 - x] = other[part].astype(jnp.bfloat16)

    def last():
        eye = lax.broadcasted_iota(jnp.int32, (rows, rows), 0) == lax.broadcasted_iota(jnp.int32, (rows, rows), 1)
        eye = jnp.where(eye, 1.0, 0.0).astype(jnp.bfloat16)
        flat = out_t[...].reshape(out_ref.shape[2], rows)
        out_ref[0] = lax.dot_general(eye, flat, NT, preferred_element_type=jnp.float32).astype(jnp.bfloat16)

    def local():
        for copy in locals_:
            copy.wait()

    work = {
        "blend": blend, "mask": mask, "attn": attn, "proj": proj, "add": add, "sum": total, "last": last, "local": local,
    }
    for verb, name in order:
        if verb == "start":
            copy_of(name, False).start()
        elif verb == "wait":
            copy_of(name, True).wait_recv()
        else:
            work[name[0]](*name[1:])
    for name in ids:
        copy_of(name, False).wait_send()


def per_device(n_y, n_z, query, key_in, value, segment_ids, blend, w_first, w_second):
    rows, width = query.shape[1], query.shape[2]
    heads = width // HEAD_DIM // 2
    half = width // 2
    patches = segment_ids.shape[1]
    piece = w_first.shape[0]
    nodes, offsets = plan(n_y, n_z, heads)
    order = order_of(nodes)
    ids = {}
    for node in nodes:
        if node.link is not None:
            ids[node.name] = len(ids)
    bf16, f32 = jnp.bfloat16, jnp.float32
    group = n_z // 4 * piece
    any_, vmem = pl.BlockSpec(memory_space=pl.ANY), pl.BlockSpec(memory_space=pltpu.VMEM)
    out_cols = 2 * n_y * group
    return pl.pallas_call(
        functools.partial(kernel, n_y, n_z, order, ids, offsets),
        out_shape=jax.ShapeDtypeStruct((1, rows, out_cols), bf16),
        in_specs=[any_, any_, any_, vmem, pl.BlockSpec(memory_space=pltpu.SMEM), vmem, vmem],
        out_specs=vmem,
        scratch_shapes=[
            pltpu.VMEM((patches, half), bf16),
            pltpu.VMEM((patches, half), bf16),
            pltpu.VMEM((2 * rows, half), bf16),
            pltpu.VMEM((2 * rows, patches), f32),
            pltpu.VMEM((n_y, n_z, piece, width), bf16),
            pltpu.VMEM((2 * heads, 2 * rows, HEAD_DIM), bf16),
            pltpu.VMEM((n_y, 2, group, 2 * rows), bf16),
            pltpu.VMEM((n_y, 2, group, 2 * rows), bf16),
            pltpu.VMEM((n_y, 2, group, 2 * rows), bf16),
            pltpu.VMEM((3, n_y, group, rows), bf16),
            pltpu.VMEM((n_y, group, rows), bf16),
            pltpu.VMEM((3, n_y, group, rows), bf16),
            pltpu.VMEM((n_z // 4, n_y, 2, piece, rows), bf16),
            pltpu.SemaphoreType.DMA((3,)),
            pltpu.SemaphoreType.DMA((len(ids),)),
            pltpu.SemaphoreType.DMA((len(ids),)),
        ],
        compiler_params=pltpu.CompilerParams(
            collective_id=0, has_side_effects=True, vmem_limit_bytes=48 * 1024 * 1024
        ),
    )(query, key_in, value, segment_ids, blend, w_first, w_second)


def solution(mesh):
    in_specs = (
        P("dp", "fsdp", "tensor"),
        P("dp", "fsdp", "tensor"),
        P("dp", "fsdp", "tensor"),
        P("dp", None),
        P(),
        P(("dp", "fsdp"), "tensor"),
        P(("dp", "fsdp"), "tensor"),
    )
    out_specs = P("dp", "fsdp", "tensor")
    body = functools.partial(per_device, mesh.shape["fsdp"] // 2, mesh.shape["dp"])
    return jax.shard_map(body, mesh=mesh, in_specs=in_specs, out_specs=out_specs, check_vma=False)
```

time: 865 us -> 82.6 us (0.10)
  waiting for transfers between devices: 822 us -> 0 us
  Pallas kernels: 0 us -> 74.9 us
  matrix products: 19 us -> 0 us
  between operations: 13.8 us -> 0.67 us
    all_gather x3 -> x0, waiting for transfers between devices: 694 us -> none  [the longest x1 520 us: per_device(): lax.all_gather(blended, ('dp', 'fsdp'), axis=0, tiled=True)]
    reduce_scatter x1 -> x0, waiting for transfers between devices: 126 us -> none  [per_device(): lax.psum_scatter(partial_value.astype(jnp.float32).astype(jnp.bfloat16),...]
    pallas_call x0 -> x1, Pallas kernels: none -> 74.9 us  [per_device(): pl.pallas_call(functools.partial(kernel, n_y, n_z, order, ids, offsets),...]
    dot_general x2 -> x0, matrix products: 11.9 us -> none  [the longest x1 8.04 us: per_device(): lax.dot_general(attended, lax.all_gather(blended, ('dp', 'fsdp'), axis=0,...]
  transfers between devices with their start and end apart: 4 -> 0, of which waited for: 4 -> 0; matrix products, arithmetic and copies ran while one was open for 2% -> 0% of each run, Pallas kernels for 0% -> 0%
where the time goes in v1:
time: 82.6 us; the launch traced here: 81.6 us
  Pallas kernels  74.9 us (91%)
  local copies, waits for them, and re-layouts  5.98 us (7%)
    pallas_call x1, Pallas kernels, per_device(): pl.pallas_call(functools.partial(kernel, n_y, n_z, order, ids, offsets),...  74.9 us
    unnamed x13, local copies, waits for them, and re-layouts  5.98 us

profile of v1, /device:TPU:1, one launch (start us, length us, event | category | flops | bytes accessed | tf_op | source)
XLA Modules:
  0.0 81.6 jit_solution(4668822892114607548)
XLA Ops:
  0.7 0.0 copy-start
  0.7 0.9 %copy-done = bf16[1,128,768]{2,1,0:T(8,128)(2,1)S(1)} copy-done((bf16[1,128,768]{2,1,0:T(8,128)(2,1)S(1)}, bf16[1,128,768]{2,1,0:T(8,128)(2,1)}, u32[]{:S(2)}) %copy-start) | copy-done | bytes 196632
  1.6 0.0 copy-start.1
  1.6 0.9 %copy-done.1 = bf16[1,128,768]{2,1,0:T(8,128)(2,1)S(1)} copy-done((bf16[1,128,768]{2,1,0:T(8,128)(2,1)S(1)}, bf16[1,128,768]{2,1,0:T(8,128)(2,1)}, u32[]{:S(2)}) %copy-start.1) | copy-done | bytes 196632
  2.5 0.0 copy-start.2
  2.5 0.9 %copy-done.2 = bf16[1,128,768]{2,1,0:T(8,128)(2,1)S(1)} copy-done((bf16[1,128,768]{2,1,0:T(8,128)(2,1)S(1)}, bf16[1,128,768]{2,1,0:T(8,128)(2,1)}, u32[]{:S(2)}) %copy-start.2) | copy-done | bytes 196632
  3.4 0.0 copy-start.3
  3.4 0.9 %copy-done.3 = bf16[48,768]{1,0:T(8,128)(2,1)S(1)} copy-done((bf16[48,768]{1,0:T(8,128)(2,1)S(1)}, bf16[48,768]{1,0:T(8,128)(2,1)}, u32[]{:S(2)}) %copy-start.3) | copy-done | bytes 73752
  4.3 0.0 copy-start.4
  4.3 0.9 %copy-done.4 = bf16[48,768]{1,0:T(8,128)(2,1)S(1)} copy-done((bf16[48,768]{1,0:T(8,128)(2,1)S(1)}, bf16[48,768]{1,0:T(8,128)(2,1)}, u32[]{:S(2)}) %copy-start.4) | copy-done | bytes 73752
  5.2 0.0 copy-start.5
  5.2 0.7 copy-done.5
  5.9 74.9 %shard_map.73 = bf16[1,128,1536]{2,1,0:T(8,128)(2,1)S(1)} custom-call(bf16[1,128,768]{2,1,0:T(8,128)(2,1)S(1)} %copy-done, bf16[1,128,768]{2,1,0:T(8,128)(2,1)S(1)} %copy-done.1, bf16[1,128,768]{2,1,0:T(8,128)(2,1)S(1)} %copy-done.2, s32[1,2048]{1,0:T(1,128)S(1)} %copy-done.5, f32[1]{0:T(128)S(6)} %copy.9.blend_ref, bf16[48,768]{1,0:T(8,128)(2,1)S(1)} %copy-done.3, ...), custom_call_target="tpu_custom_call" | custom-call | tf_op jit(solution)/shard_map/pallas_call | solution.py:328
  80.8 0.7 copy.10
Async XLA Ops:
  0.7 0.9 %copy-start = (bf16[1,128,768]{2,1,0:T(8,128)(2,1)S(1)}, bf16[1,128,768]{2,1,0:T(8,128)(2,1)}, u32[]{:S(2)}) copy-start(bf16[1,128,768]{2,1,0:T(8,128)(2,1)} %q_hbm.1) | copy-start | bytes 589828
  1.6 0.9 %copy-start.1 = (bf16[1,128,768]{2,1,0:T(8,128)(2,1)S(1)}, bf16[1,128,768]{2,1,0:T(8,128)(2,1)}, u32[]{:S(2)}) copy-start(bf16[1,128,768]{2,1,0:T(8,128)(2,1)} %k_hbm.1) | copy-start | bytes 589828
  2.5 0.9 %copy-start.2 = (bf16[1,128,768]{2,1,0:T(8,128)(2,1)S(1)}, bf16[1,128,768]{2,1,0:T(8,128)(2,1)}, u32[]{:S(2)}) copy-start(bf16[1,128,768]{2,1,0:T(8,128)(2,1)} %v_hbm.1) | copy-start | bytes 589828
  3.4 0.9 %copy-start.3 = (bf16[48,768]{1,0:T(8,128)(2,1)S(1)}, bf16[48,768]{1,0:T(8,128)(2,1)}, u32[]{:S(2)}) copy-start(bf16[48,768]{1,0:T(8,128)(2,1)} %w_first.1) | copy-start | bytes 221188
  4.3 0.9 %copy-start.4 = (bf16[48,768]{1,0:T(8,128)(2,1)S(1)}, bf16[48,768]{1,0:T(8,128)(2,1)}, u32[]{:S(2)}) copy-start(bf16[48,768]{1,0:T(8,128)(2,1)} %w_second.1) | copy-start | bytes 221188
  5.2 0.7 copy-start.5

commit v2 on v1

--- a/solution.py
+++ b/solution.py
@@ -9,6 +9,9 @@
 from jax.sharding import PartitionSpec as P
 
 HEAD_DIM = 128
+LAST = 256
+IDLE = 4
+WINDOW = 6
 MESH = pl.DeviceIdType.MESH
 NT = (((1,), (1,)), ((), ()))
 
@@ -18,7 +21,7 @@
         self.name, self.deps, self.cost, self.link, self.rank = name, list(deps), cost, link, rank
 
 
-def order_of(nodes, latency=1.5):
+def order_of(nodes, latency=2.0):
     by_name = {node.name: node for node in nodes}
     position = {node.name: i for i, node in enumerate(nodes)}
     feeds = {node.name: False for node in nodes}
@@ -28,6 +31,7 @@
                 feeds[dep] = True
     done, started, waited = set(), set(), set()
     arrivals, free, order, now = [], {}, [], 0.0
+    flying = []
     while len(done) < len(nodes):
         for node in nodes:
             if node.link is not None and node.name not in started and all(d in done for d in node.deps):
@@ -40,6 +44,7 @@
                 begin = max(now, free.get(node.link, 0.0))
                 free[node.link] = begin + node.cost
                 heapq.heappush(arrivals, (begin + node.cost + latency, position[node.name], node.name))
+                flying.append((begin + node.cost + latency, node.name))
         if arrivals and arrivals[0][0] <= now:
             name = heapq.heappop(arrivals)[2]
             done.add(name)
@@ -58,8 +63,12 @@
             now += node.cost
             done.add(node.name)
             continue
+        for item in sorted(flying)[:IDLE]:
+            if item[0] + 1.0 < now:
+                flying.remove(item)
+                order.append(("sent", item[1]))
         now = max(now, arrivals[0][0])
-    return order
+    return order + [("sent", name) for _, name in sorted(flying)]
 
 
 def plan(n_y, n_z, heads):
@@ -69,7 +78,7 @@
         nodes.append(Node(name, deps, cost, link, rank))
         return name
 
-    w_cost, kv_cost = 1.5, 2.0
+    w_cost, kv_cost = 1.6, 1.4
     offsets = [0]
     for k in range(1, n_y // 2 + 1):
         offsets += [-k, k] if 2 * k < n_y else [-k]
@@ -82,38 +91,56 @@
         add(("wy", j), [("wy", j - sign)] if abs(j) > 1 else [("blend",)], w_cost, link)
     for slot, j in enumerate(offsets):
         source = ("wy", j) if j else ("blend",)
+        cost = w_cost * (1 - LAST / 768 if abs(j) == 1 else 1)
         up = n_z // 2 - (slot % 2)
         for k in range(1, n_z // 2 + 1):
             for way, most in ((1, up), (-1, n_z - 1 - up)):
                 if k <= most:
                     link = "z+" if way > 0 else "z-"
-                    add(("wz", slot, way * k), [("wz", slot, way * (k - 1))] if k > 1 else [source], w_cost, link)
+                    add(("wz", slot, way * k), [("wz", slot, way * (k - 1))] if k > 1 else [source], cost, link)
     add(("local",), [], 0.5, rank=-2)
-    for part in ("k", "v", "q"):
-        add(("x", part), [], kv_cost, "x")
-    for part, up in (("k", n_y // 2), ("v", n_y - 1 - n_y // 2)):
-        for own in (1, 0):
-            source = ("local",) if own else ("x", part)
-            for k in range(1, n_y // 2 + 1):
-                for way, most in ((1, up), (-1, n_y - 1 - up)):
-                    if k <= most:
-                        link = "y+" if way > 0 else "y-"
-                        add((part, own, way * k), [(part, own, way * (k - 1))] if k > 1 else [source], kv_cost, link)
+    for h in range(heads):
+        for i in range(2):
+            add(("x", h, i), [], kv_cost / 2, "x")
+    add(("xq",), [], kv_cost, "x")
+    streams = [(h, own) for h in range(heads) for own in (1, 0)]
+    hops = {1: (n_y // 2, n_y - 1 - n_y // 2), 0: (n_y - 1 - n_y // 2, n_y // 2)}
+    for i, (h, own) in enumerate(streams):
+        source = [("local",)] if own else [("x", h, 0), ("x", h, 1)]
+        for k in range(1, n_y // 2 + 1):
+            for way, most in zip((1, -1), hops[own]):
+                if k <= most:
+                    deps = [("kv", h, own, way * (k - 1))] if k > 1 else list(source)
+                    if k == 1 and i >= WINDOW:
+                        before = streams[i - WINDOW]
+                        deps.append(("kv", *before, way * (hops[before[1]][way < 0] - 1)))
+                    add(("kv", h, own, way * k), deps, kv_cost, "y+" if way > 0 else "y-")
+    if LAST:
+        gathered = [n.name for n in nodes if n.name[:2] == ("wz", 0)]
+        for j in (-1, 1):
+            late = [("kv", h, own, -j * hops[own][j > 0]) for h, own in streams]
+            add(("yl", j), gathered + late, 13.0 * LAST / 768, "y+" if j < 0 else "y-")
     add(("mask",), [], 1.0, rank=-1)
-    held = [("mask",), ("local",)] + [n.name for n in nodes if n.name[0] in ("k", "v", "x")]
     for h in range(heads):
+        held = [("mask",), ("local",), ("x", h, 0), ("x", h, 1), ("xq",)]
+        rest = [n.name for n in nodes if n.name[:2] == ("kv", h) and 2 * abs(n.name[3]) == n_y]
+        held += [n.name for n in nodes if n.name[:2] == ("kv", h) and 2 * abs(n.name[3]) < n_y]
         for half in range(2):
-            add(("attn", h, half), held, 0.8)
-        add(("a", h), [("attn", h, 0), ("attn", h, 1)], 1.3, "x")
-    ready = [("a", h) for h in range(heads)]
+            add(("near", h, half), held, 0.5)
+            add(("far", h, half), [("near", h, half)] + rest, 0.15, rank=-5)
+            add(("a", h, half), [("far", h, half)], 0.7, "x")
+    ready = [("a", h, half) for h in range(heads) for half in range(2)]
     for slot, j in enumerate(offsets):
         shards = [n.name for n in nodes if n.name[0] == "wz" and n.name[1] == slot]
-        source = ("wy", j) if j else ("blend",)
-        add(("proj", slot), ready + shards + [source], 0.4, rank=slot)
+        source = [("wy", j)] if j else [("blend",)]
+        if LAST and abs(j) == 1:
+            source.append(("yl", j))
+        add(("pre", slot), ready[:-2] + shards + source, 0.35, rank=slot + 30)
+        add(("proj", slot), ready[-2:] + [("pre", slot)], 0.2, rank=slot)
         add(("c", slot), [("proj", slot)], 0.3, "core")
         add(("add", slot), [("c", slot)], 0.1, rank=slot - 20)
         for r in range(3):
-            add(("e", slot, r), [("add", slot)], 0.5 if r else 1.0, "x")
+            add(("e", slot, r), [("add", slot)], 1.0, "x%d" % r)
         add(("sum", slot), [("e", slot, r) for r in range(3)], 0.1, rank=slot + 20)
     add(("last",), [("sum", slot) for slot in range(n_y)], 0.5, rank=100)
     return nodes, offsets
@@ -122,7 +149,7 @@
 def kernel(
     n_y, n_z, order, ids, offsets,
     q_hbm, k_hbm, v_hbm, seg_ref, blend_ref, w_first, w_second, out_ref,
-    kbuf, vbuf, qbuf, bias, wbuf, attbuf, p_own, p_send, c_recv, s_send, s_keep, e_recv, out_t,
+    kvbuf, qbuf, bias, stats, wbuf, attbuf, acc, p_all, c_recv, s_send, s_keep, e_recv, out_t,
     local_sem, send_sem, recv_sem,
 ):
     z = lax.axis_index("dp")
@@ -131,18 +158,22 @@
     y, x = f // 2, f % 2
     x_hi, core = t // 2, t % 2
     rows = q_hbm.shape[1]
-    half_width = kbuf.shape[1]
+    half_width = q_hbm.shape[2] // 2
     heads = half_width // HEAD_DIM
     piece = w_first.shape[0]
+    split = w_first.shape[1] - LAST
     x_other = f + 1 - 2 * x
     t_core = t + 1 - 2 * core
     t_hi = t + 2 - 4 * x_hi
 
+    ys = [(y + d) % n_y for d in range(n_y)]
+    zs = [(z + d) % n_z for d in range(n_z)]
+
     def y_at(d):
-        return (y + d + 2 * n_y) % n_y
+        return ys[d % n_y]
 
     def z_at(d):
-        return (z + d + 2 * n_z) % n_z
+        return zs[d % n_z]
 
     def to(dp=None, fsdp=None, tensor=None):
         return (z if dp is None else dp, f if fsdp is None else fsdp, t if tensor is None else tensor)
@@ -164,16 +195,20 @@
     def token_rows(y_index, x_index):
         return pl.ds(pl.multiple_of((y_index * 2 + x_index) * rows, rows), rows)
 
-    bufs = {"k": kbuf, "v": vbuf, "q": qbuf}
-    hbm = {"k": k_hbm, "v": v_hbm, "q": q_hbm}
+    def head_of(x_index, h):
+        return pl.ds(pl.multiple_of((x_index * heads + h) * HEAD_DIM, HEAD_DIM), HEAD_DIM)
 
     def q_rows(x_index):
         return pl.ds(pl.multiple_of(x_index * rows, rows), rows)
 
-    locals_ = []
-    for i, part in enumerate(("k", "v", "q")):
-        at = q_rows(x) if part == "q" else token_rows(y, x)
-        locals_.append(pltpu.make_async_copy(hbm[part].at[0, :, mine], bufs[part].at[at], local_sem.at[i]))
+    locals_ = [pltpu.make_async_copy(q_hbm.at[0, :, mine], qbuf.at[q_rows(x)], local_sem.at[0])]
+    for h in range(heads):
+        for i, source in enumerate((k_hbm, v_hbm)):
+            locals_.append(
+                pltpu.make_async_copy(
+                    source.at[0, :, head_of(x, h)], kvbuf.at[h, i, token_rows(y, x)], local_sem.at[1 + 2 * h + i]
+                )
+            )
     for copy in locals_:
         copy.start()
 
@@ -193,28 +228,36 @@
             slot, k = name[1:]
             way = 1 if k > 0 else -1
             src = dst = wbuf.at[y_at(offsets[slot]), z_at(-k if arriving else -(k - way))]
+            if abs(offsets[slot]) == 1 and LAST:
+                src = dst = src.at[:, :split]
             who = to(dp=z_at(way))
+        elif kind == "yl":
+            j = name[1]
+            src = dst = wbuf.at[y_at(j if arriving else 0), :, :, split:]
+            who = to(fsdp=y_at(-j) * 2 + x)
+        elif kind == "xq":
+            dst = qbuf.at[q_rows(1 - x if arriving else x)]
+            src = dst if arriving else q_hbm.at[0, :, theirs]
+            who = to(fsdp=x_other)
         elif kind == "x":
-            part = name[1]
-            from_x = 1 - x if arriving else x
-            at = q_rows(from_x) if part == "q" else token_rows(y, from_x)
-            dst = bufs[part].at[at]
-            src = dst if arriving else hbm[part].at[0, :, theirs]
+            h, i = name[1:]
+            dst = kvbuf.at[h, i, token_rows(y, 1 - x if arriving else x)]
+            src = dst if arriving else (k_hbm, v_hbm)[i].at[0, :, head_of(1 - x, h)]
             who = to(fsdp=x_other)
-        elif kind in ("k", "v"):
-            own, k = name[1:]
+        elif kind == "kv":
+            h, own, k = name[1:]
             way = 1 if k > 0 else -1
             part_x = x if own else 1 - x
-            src = dst = bufs[kind].at[token_rows(y_at(-k if arriving else -(k - way)), part_x)]
+            src = dst = kvbuf.at[h, :, token_rows(y_at(-k if arriving else -(k - way)), part_x)]
             who = to(fsdp=y_at(way) * 2 + x)
         elif kind == "a":
-            h = name[1]
-            src = dst = attbuf.at[((1 - x) if arriving else x) * heads + h]
+            h, half = name[1:]
+            src = dst = attbuf.at[((1 - x) if arriving else x) * heads + h, half * rows : (half + 1) * rows]
             who = to(fsdp=x_other)
         elif kind == "c":
             slot = name[1]
             dst = c_recv.at[slot]
-            src = dst if arriving else p_send.at[slot]
+            src = dst if arriving else p_all.at[slot, :, 1 - core]
             who = to(tensor=t_core)
         else:
             slot, r = name[1:]
@@ -240,31 +283,53 @@
         keys = seg_ref[...].astype(jnp.float32)
         bias[...] = jnp.where(column == keys, jnp.float32(0.0), jnp.float32(-1e30))
 
-    def attn(h, half):
+    def scores_of(h, half, j):
         at, cols = slice(half * rows, (half + 1) * rows), slice(h * HEAD_DIM, (h + 1) * HEAD_DIM)
-        scores = lax.dot_general(qbuf[at, cols], kbuf[:, cols], NT, preferred_element_type=jnp.float32)
-        scores = scores * HEAD_DIM ** (-0.5) + bias[at, :]
-        top = jnp.max(scores, axis=1, keepdims=True)
-        expo = jnp.exp(scores - top)
-        total = jnp.sum(expo, axis=1, keepdims=True)
-        result = jnp.dot(expo.astype(jnp.bfloat16), vbuf[:, cols], preferred_element_type=jnp.float32)
-        attbuf[x * heads + h, at, :] = (result / total).astype(jnp.bfloat16)
+        keys = pl.ds(pl.multiple_of(y_at(j) * 2 * rows, 2 * rows), 2 * rows)
+        scores = lax.dot_general(qbuf[at, cols], kvbuf[h, 0, keys], NT, preferred_element_type=jnp.float32)
+        return scores * HEAD_DIM ** (-0.5) + bias[at, keys], keys
+
+    def near(h, half):
+        blocks = [scores_of(h, half, j) for j in range(1 - n_y // 2, n_y // 2)]
+        top = jnp.max(functools.reduce(jnp.maximum, [scores for scores, _ in blocks]), axis=1, keepdims=True)
+        expos = [jnp.exp(scores - top) for scores, _ in blocks]
+        total = jnp.sum(functools.reduce(jnp.add, expos), axis=1, keepdims=True)
+        result = jnp.zeros((rows, HEAD_DIM), jnp.float32)
+        for expo, (_, keys) in zip(expos, blocks):
+            result += jnp.dot(expo.astype(jnp.bfloat16), kvbuf[h, 1, keys], preferred_element_type=jnp.float32)
+        stats[h, half, 0] = jnp.broadcast_to(top, (rows, HEAD_DIM))
+        stats[h, half, 1] = jnp.broadcast_to(total, (rows, HEAD_DIM))
+        stats[h, half, 2] = result
+
+    def far(h, half):
+        scores, keys = scores_of(h, half, n_y // 2)
+        before = stats[h, half, 0][:, :1]
+        top = jnp.maximum(before, jnp.max(scores, axis=1, keepdims=True))
+        expo, shrink = jnp.exp(scores - top), jnp.exp(before - top)
+        total = stats[h, half, 1][:, :1] * shrink + jnp.sum(expo, axis=1, keepdims=True)
+        result = jnp.dot(expo.astype(jnp.bfloat16), kvbuf[h, 1, keys], preferred_element_type=jnp.float32)
+        result = (stats[h, half, 2] * shrink + result) / total
+        attbuf[x * heads + h, half * rows : (half + 1) * rows, :] = result.astype(jnp.bfloat16)
+
+    def product(slot, spans):
+        at = y_at(offsets[slot])
+        weight = jnp.concatenate(
+            [wbuf[at, :, :, a * HEAD_DIM : b * HEAD_DIM].reshape(n_z * piece, (b - a) * HEAD_DIM) for a, b in spans], axis=1
+        )
+        attended = jnp.concatenate([attbuf[i] for a, b in spans for i in range(a, b)], axis=1)
+        return lax.dot_general(weight, attended, NT, preferred_element_type=jnp.float32)
+
+    def pre(slot):
+        acc[slot] = product(slot, [(0, heads - 1), (heads, 2 * heads - 1)])
 
     def proj(slot):
-        attended = jnp.concatenate([attbuf[i] for i in range(2 * heads)], axis=1)
-        shards = wbuf.at[y_at(offsets[slot])]
-        per = n_z // 4
-        for hi in range(2):
-            for same in range(2):
-                first = (hi * 2 + (core if same else 1 - core)) * per
-                weight = shards[pl.ds(first, per)].reshape(per * piece, attended.shape[1])
-                part = lax.dot_general(weight, attended, NT, preferred_element_type=jnp.float32).astype(jnp.bfloat16)
-                (p_own if same else p_send)[slot, hi] = part
+        part = acc[slot] + product(slot, [(heads - 1, heads), (2 * heads - 1, 2 * heads)])
+        p_all[slot] = part.astype(jnp.bfloat16).reshape(p_all.shape[1:])
 
     def add(slot):
         for away in range(2):
             hi = (1 - x_hi) if away else x_hi
-            both = (p_own[slot, hi].astype(jnp.float32) + c_recv[slot, hi].astype(jnp.float32)).astype(jnp.bfloat16)
+            both = (p_all[slot, hi, core].astype(jnp.float32) + c_recv[slot, hi].astype(jnp.float32)).astype(jnp.bfloat16)
             first, second = both[:, :rows], both[:, rows:]
             keep = jnp.where(x == 0, first, second)
             move = jnp.where(x == 0, second, first)
@@ -296,17 +361,17 @@
             copy.wait()
 
     work = {
-        "blend": blend, "mask": mask, "attn": attn, "proj": proj, "add": add, "sum": total, "last": last, "local": local,
+        "blend": blend, "mask": mask, "near": near, "far": far, "pre": pre, "proj": proj, "add": add, "sum": total, "last": last, "local": local,
     }
     for verb, name in order:
         if verb == "start":
             copy_of(name, False).start()
         elif verb == "wait":
             copy_of(name, True).wait_recv()
+        elif verb == "sent":
+            copy_of(name, False).wait_send()
         else:
             work[name[0]](*name[1:])
-    for name in ids:
-        copy_of(name, False).wait_send()
 
 
 def per_device(n_y, n_z, query, key_in, value, segment_ids, blend, w_first, w_second):
@@ -331,25 +396,25 @@
         in_specs=[any_, any_, any_, vmem, pl.BlockSpec(memory_space=pltpu.SMEM), vmem, vmem],
         out_specs=vmem,
         scratch_shapes=[
-            pltpu.VMEM((patches, half), bf16),
-            pltpu.VMEM((patches, half), bf16),
+            pltpu.VMEM((heads, 2, patches, HEAD_DIM), bf16),
             pltpu.VMEM((2 * rows, half), bf16),
             pltpu.VMEM((2 * rows, patches), f32),
+            pltpu.VMEM((heads, 2, 3, rows, HEAD_DIM), f32),
             pltpu.VMEM((n_y, n_z, piece, width), bf16),
             pltpu.VMEM((2 * heads, 2 * rows, HEAD_DIM), bf16),
-            pltpu.VMEM((n_y, 2, group, 2 * rows), bf16),
-            pltpu.VMEM((n_y, 2, group, 2 * rows), bf16),
+            pltpu.VMEM((n_y, n_z * piece, 2 * rows), f32),
+            pltpu.VMEM((n_y, 2, 2, group, 2 * rows), bf16),
             pltpu.VMEM((n_y, 2, group, 2 * rows), bf16),
             pltpu.VMEM((3, n_y, group, rows), bf16),
             pltpu.VMEM((n_y, group, rows), bf16),
             pltpu.VMEM((3, n_y, group, rows), bf16),
             pltpu.VMEM((n_z // 4, n_y, 2, piece, rows), bf16),
-            pltpu.SemaphoreType.DMA((3,)),
+            pltpu.SemaphoreType.DMA((1 + 2 * heads,)),
             pltpu.SemaphoreType.DMA((len(ids),)),
             pltpu.SemaphoreType.DMA((len(ids),)),
         ],
         compiler_params=pltpu.CompilerParams(
-            collective_id=0, has_side_effects=True, vmem_limit_bytes=48 * 1024 * 1024
+            collective_id=0, has_side_effects=True, vmem_limit_bytes=62 * 1024 * 1024
         ),
     )(query, key_in, value, segment_ids, blend, w_first, w_second)
 

time: 82.6 us -> 75.6 us (0.915)
  local copies, waits for them, and re-layouts: 5.98 us -> 1.77 us
  Pallas kernels: 74.9 us -> 72.3 us
    unnamed x13 -> x1, local copies, waits for them, and re-layouts: 5.98 us -> 1.77 us
    pallas_call x1, Pallas kernels: 74.9 us -> 72.3 us  [per_device(): pl.pallas_call(functools.partial(kernel, n_y, n_z, order, ids, offsets),...]
where the time goes in v2:
time: 75.6 us; the launch traced here: 74.7 us
  Pallas kernels  72.3 us (96%)
  local copies, waits for them, and re-layouts  1.77 us (2%)
    pallas_call x1, Pallas kernels, per_device(): pl.pallas_call(functools.partial(kernel, n_y, n_z, order, ids, offsets),...  72.3 us
    unnamed x1, local copies, waits for them, and re-layouts  1.77 us

profile of v2, /device:TPU:1, one launch (start us, length us, event | category | flops | bytes accessed | tf_op | source)
XLA Modules:
  0.0 74.7 jit_solution(8726982944655982461)
XLA Ops:
  0.7 72.3 %shard_map.73 = bf16[1,128,1536]{2,1,0:T(8,128)(2,1)} custom-call(bf16[1,128,768]{2,1,0:T(8,128)(2,1)} %q_hbm.1, bf16[1,128,768]{2,1,0:T(8,128)(2,1)} %k_hbm.1, bf16[1,128,768]{2,1,0:T(8,128)(2,1)} %v_hbm.1, s32[1,2048]{1,0:T(1,128)} %seg_ref.1, f32[1]{0:T(128)S(6)} %copy.9.blend_ref, bf16[48,768]{1,0:T(8,128)(2,1)} %w_first.1, bf16[48,768]{1,0:T(8,128)(2,1)} %w_second.1), custom_call_target="tpu_custom_call" | custom-call | tf_op jit(solution)/shard_map/pallas_call | solution.py:393
  73.0 1.8 %copy.10 = bf16[1,128,1536]{2,1,0:T(8,128)(2,1)} copy(bf16[1,128,1536]{2,1,0:T(8,128)(2,1)} %shard_map.73) | data formatting | bytes 786432

commit v3 on v2

--- a/solution.py
+++ b/solution.py
@@ -12,6 +12,8 @@
 LAST = 256
 IDLE = 4
 WINDOW = 6
+LATENCY, LATENCY_ELSE = {"y": 1.92, "z": 1.78}, 2.04
+SHARD_US, BLOCK_US = 1.558, 1.335
 MESH = pl.DeviceIdType.MESH
 NT = (((1,), (1,)), ((), ()))
 
@@ -21,7 +23,7 @@
         self.name, self.deps, self.cost, self.link, self.rank = name, list(deps), cost, link, rank
 
 
-def order_of(nodes, latency=2.0):
+def order_of(nodes):
     by_name = {node.name: node for node in nodes}
     position = {node.name: i for i, node in enumerate(nodes)}
     feeds = {node.name: False for node in nodes}
@@ -43,8 +45,9 @@
                 order.append(("start", node.name))
                 begin = max(now, free.get(node.link, 0.0))
                 free[node.link] = begin + node.cost
-                heapq.heappush(arrivals, (begin + node.cost + latency, position[node.name], node.name))
-                flying.append((begin + node.cost + latency, node.name))
+                landing = begin + node.cost + LATENCY.get(node.link[0], LATENCY_ELSE)
+                heapq.heappush(arrivals, (landing, position[node.name], node.name))
+                flying.append((landing, node.name))
         if arrivals and arrivals[0][0] <= now:
             name = heapq.heappop(arrivals)[2]
             done.add(name)
@@ -78,7 +81,7 @@
         nodes.append(Node(name, deps, cost, link, rank))
         return name
 
-    w_cost, kv_cost = 1.6, 1.4
+    w_cost, kv_cost = SHARD_US, BLOCK_US
     offsets = [0]
     for k in range(1, n_y // 2 + 1):
         offsets += [-k, k] if 2 * k < n_y else [-k]
@@ -126,7 +129,7 @@
         rest = [n.name for n in nodes if n.name[:2] == ("kv", h) and 2 * abs(n.name[3]) == n_y]
         held += [n.name for n in nodes if n.name[:2] == ("kv", h) and 2 * abs(n.name[3]) < n_y]
         for half in range(2):
-            add(("near", h, half), held, 0.5)
+            add(("near", h, half), held, 0.45)
             add(("far", h, half), [("near", h, half)] + rest, 0.15, rank=-5)
             add(("a", h, half), [("far", h, half)], 0.7, "x")
     ready = [("a", h, half) for h in range(heads) for half in range(2)]
@@ -148,8 +151,8 @@
 
 def kernel(
     n_y, n_z, order, ids, offsets,
-    q_hbm, k_hbm, v_hbm, seg_ref, blend_ref, w_first, w_second, out_ref,
-    kvbuf, qbuf, bias, stats, wbuf, attbuf, acc, p_all, c_recv, s_send, s_keep, e_recv, out_t,
+    q_hbm, k_hbm, v_hbm, seg_hbm, blend_ref, first_hbm, second_hbm, out_ref,
+    seg_ref, w_in, kvbuf, qbuf, bias, stats, wbuf, attbuf, acc, p_all, c_recv, s_send, s_keep, e_recv, out_t,
     local_sem, send_sem, recv_sem,
 ):
     z = lax.axis_index("dp")
@@ -160,8 +163,7 @@
     rows = q_hbm.shape[1]
     half_width = q_hbm.shape[2] // 2
     heads = half_width // HEAD_DIM
-    piece = w_first.shape[0]
-    split = w_first.shape[1] - LAST
+    piece, split = w_in.shape[1], w_in.shape[2] - LAST
     x_other = f + 1 - 2 * x
     t_core = t + 1 - 2 * core
     t_hi = t + 2 - 4 * x_hi
@@ -201,6 +203,11 @@
     def q_rows(x_index):
         return pl.ds(pl.multiple_of(x_index * rows, rows), rows)
 
+    weights = [
+        pltpu.make_async_copy(first_hbm, w_in.at[0], local_sem.at[1 + 2 * heads]),
+        pltpu.make_async_copy(second_hbm, w_in.at[1], local_sem.at[2 + 2 * heads]),
+    ]
+    ids_copy = pltpu.make_async_copy(seg_hbm, seg_ref, local_sem.at[3 + 2 * heads])
     locals_ = [pltpu.make_async_copy(q_hbm.at[0, :, mine], qbuf.at[q_rows(x)], local_sem.at[0])]
     for h in range(heads):
         for i, source in enumerate((k_hbm, v_hbm)):
@@ -209,7 +216,7 @@
                     source.at[0, :, head_of(x, h)], kvbuf.at[h, i, token_rows(y, x)], local_sem.at[1 + 2 * h + i]
                 )
             )
-    for copy in locals_:
+    for copy in weights + locals_ + [ids_copy]:
         copy.start()
 
     barrier = pltpu.get_barrier_semaphore()
@@ -271,11 +278,14 @@
         )
 
     def blend():
+        for copy in weights:
+            copy.wait()
         coef = blend_ref[0]
-        mixed = (1.0 - coef) * w_first[...].astype(jnp.float32) + coef * w_second[...].astype(jnp.float32)
+        mixed = (1.0 - coef) * w_in[0].astype(jnp.float32) + coef * w_in[1].astype(jnp.float32)
         wbuf[y, z] = mixed.astype(jnp.bfloat16)
 
     def mask():
+        ids_copy.wait()
         count = 2 * rows
         row = seg_ref[:, pl.ds(pl.multiple_of(y * count, count), count)].astype(jnp.float32)
         on = lax.broadcasted_iota(jnp.int32, (count, count), 0) == lax.broadcasted_iota(jnp.int32, (count, count), 1)
@@ -393,9 +403,11 @@
     return pl.pallas_call(
         functools.partial(kernel, n_y, n_z, order, ids, offsets),
         out_shape=jax.ShapeDtypeStruct((1, rows, out_cols), bf16),
-        in_specs=[any_, any_, any_, vmem, pl.BlockSpec(memory_space=pltpu.SMEM), vmem, vmem],
+        in_specs=[any_, any_, any_, any_, pl.BlockSpec(memory_space=pltpu.SMEM), any_, any_],
         out_specs=vmem,
         scratch_shapes=[
+            pltpu.VMEM((1, patches), jnp.int32),
+            pltpu.VMEM((2, piece, width), bf16),
             pltpu.VMEM((heads, 2, patches, HEAD_DIM), bf16),
             pltpu.VMEM((2 * rows, half), bf16),
             pltpu.VMEM((2 * rows, patches), f32),
@@ -409,7 +421,7 @@
             pltpu.VMEM((n_y, group, rows), bf16),
             pltpu.VMEM((3, n_y, group, rows), bf16),
             pltpu.VMEM((n_z // 4, n_y, 2, piece, rows), bf16),
-            pltpu.SemaphoreType.DMA((1 + 2 * heads,)),
+            pltpu.SemaphoreType.DMA((4 + 2 * heads,)),
             pltpu.SemaphoreType.DMA((len(ids),)),
             pltpu.SemaphoreType.DMA((len(ids),)),
         ],

time: 75.6 us -> 74.2 us (0.981)
  no operation moved by 1% of the time
where the time goes in v3:
time: 74.2 us; the launch traced here: 74 us
  Pallas kernels  71.6 us (96%)
  local copies, waits for them, and re-layouts  1.77 us (2%)
    pallas_call x1, Pallas kernels, per_device(): pl.pallas_call(functools.partial(kernel, n_y, n_z, order, ids, offsets),...  71.6 us
    unnamed x1, local copies, waits for them, and re-layouts  1.77 us

profile of v3, /device:TPU:1, one launch (start us, length us, event | category | flops | bytes accessed | tf_op | source)
XLA Modules:
  0.0 74.0 jit_solution(4272730327162779579)
XLA Ops:
  0.7 71.6 %shard_map.73 = bf16[1,128,1536]{2,1,0:T(8,128)(2,1)} custom-call(bf16[1,128,768]{2,1,0:T(8,128)(2,1)} %q_hbm.1, bf16[1,128,768]{2,1,0:T(8,128)(2,1)} %k_hbm.1, bf16[1,128,768]{2,1,0:T(8,128)(2,1)} %v_hbm.1, s32[1,2048]{1,0:T(1,128)} %seg_hbm.1, f32[1]{0:T(128)S(6)} %copy.9.blend_ref, bf16[48,768]{1,0:T(8,128)(2,1)} %first_hbm.1, bf16[48,768]{1,0:T(8,128)(2,1)} %second_hbm.1), custom_call_target="tpu_custom_call" | custom-call | tf_op jit(solution)/shard_map/pallas_call | solution.py:403
  72.2 1.8 %copy.10 = bf16[1,128,1536]{2,1,0:T(8,128)(2,1)} copy(bf16[1,128,1536]{2,1,0:T(8,128)(2,1)} %shard_map.73) | data formatting | bytes 786432

commit v4 on v3

--- a/solution.py
+++ b/solution.py
@@ -12,8 +12,8 @@
 LAST = 256
 IDLE = 4
 WINDOW = 6
-LATENCY, LATENCY_ELSE = {"y": 1.92, "z": 1.78}, 2.04
-SHARD_US, BLOCK_US = 1.558, 1.335
+LATENCY, LATENCY_ELSE = {"y": 2.04, "z": 1.97}, 2.21
+SHARD_US, BLOCK_US = 1.558, 1.346
 MESH = pl.DeviceIdType.MESH
 NT = (((1,), (1,)), ((), ()))
 
@@ -129,7 +129,7 @@
         rest = [n.name for n in nodes if n.name[:2] == ("kv", h) and 2 * abs(n.name[3]) == n_y]
         held += [n.name for n in nodes if n.name[:2] == ("kv", h) and 2 * abs(n.name[3]) < n_y]
         for half in range(2):
-            add(("near", h, half), held, 0.45)
+            add(("near", h, half), held, 0.56)
             add(("far", h, half), [("near", h, half)] + rest, 0.15, rank=-5)
             add(("a", h, half), [("far", h, half)], 0.7, "x")
     ready = [("a", h, half) for h in range(heads) for half in range(2)]

time: 74.2 us -> 73.7 us (level)
  no operation moved by 1% of the time
where the time goes in v4:
time: 73.7 us; the launch traced here: 73.3 us
  Pallas kernels  70.9 us (96%)
  local copies, waits for them, and re-layouts  1.77 us (2%)
    pallas_call x1, Pallas kernels, per_device(): pl.pallas_call(functools.partial(kernel, n_y, n_z, order, ids, offsets),...  70.9 us
    unnamed x1, local copies, waits for them, and re-layouts  1.77 us

profile of v4, /device:TPU:1, one launch (start us, length us, event | category | flops | bytes accessed | tf_op | source)
XLA Modules:
  0.0 73.3 jit_solution(15631383642639701616)
XLA Ops:
  0.7 70.9 %shard_map.73 = bf16[1,128,1536]{2,1,0:T(8,128)(2,1)} custom-call(bf16[1,128,768]{2,1,0:T(8,128)(2,1)} %q_hbm.1, bf16[1,128,768]{2,1,0:T(8,128)(2,1)} %k_hbm.1, bf16[1,128,768]{2,1,0:T(8,128)(2,1)} %v_hbm.1, s32[1,2048]{1,0:T(1,128)} %seg_hbm.1, f32[1]{0:T(128)S(6)} %copy.9.blend_ref, bf16[48,768]{1,0:T(8,128)(2,1)} %first_hbm.1, bf16[48,768]{1,0:T(8,128)(2,1)} %second_hbm.1), custom_call_target="tpu_custom_call" | custom-call | tf_op jit(solution)/shard_map/pallas_call | solution.py:403
  71.5 1.8 %copy.10 = bf16[1,128,1536]{2,1,0:T(8,128)(2,1)} copy(bf16[1,128,1536]{2,1,0:T(8,128)(2,1)} %shard_map.73) | data formatting | bytes 786432

commit v5 on v4

--- a/solution.py
+++ b/solution.py
@@ -12,8 +12,8 @@
 LAST = 256
 IDLE = 4
 WINDOW = 6
-LATENCY, LATENCY_ELSE = {"y": 2.04, "z": 1.97}, 2.21
-SHARD_US, BLOCK_US = 1.558, 1.346
+LATENCY, LATENCY_ELSE = {"y": 2.01, "z": 1.98}, 2.1
+SHARD_US, BLOCK_US = 1.541, 1.353
 MESH = pl.DeviceIdType.MESH
 NT = (((1,), (1,)), ((), ()))
 
@@ -129,7 +129,7 @@
         rest = [n.name for n in nodes if n.name[:2] == ("kv", h) and 2 * abs(n.name[3]) == n_y]
         held += [n.name for n in nodes if n.name[:2] == ("kv", h) and 2 * abs(n.name[3]) < n_y]
         for half in range(2):
-            add(("near", h, half), held, 0.56)
+            add(("near", h, half), held, 0.6)
             add(("far", h, half), [("near", h, half)] + rest, 0.15, rank=-5)
             add(("a", h, half), [("far", h, half)], 0.7, "x")
     ready = [("a", h, half) for h in range(heads) for half in range(2)]

time: 73.7 us -> 74.2 us (level)
    pallas_call x1, Pallas kernels: 70.9 us -> 71.6 us  [per_device(): pl.pallas_call(functools.partial(kernel, n_y, n_z, order, ids, offsets),...]
where the time goes in v5:
time: 74.2 us; the launch traced here: 74.1 us
  Pallas kernels  71.6 us (96%)
  local copies, waits for them, and re-layouts  1.77 us (2%)
    pallas_call x1, Pallas kernels, per_device(): pl.pallas_call(functools.partial(kernel, n_y, n_z, order, ids, offsets),...  71.6 us
    unnamed x1, local copies, waits for them, and re-layouts  1.77 us

profile of v5, /device:TPU:1, one launch (start us, length us, event | category | flops | bytes accessed | tf_op | source)
XLA Modules:
  0.0 74.1 jit_solution(334141972631146691)
XLA Ops:
  0.7 71.6 %shard_map.73 = bf16[1,128,1536]{2,1,0:T(8,128)(2,1)} custom-call(bf16[1,128,768]{2,1,0:T(8,128)(2,1)} %q_hbm.1, bf16[1,128,768]{2,1,0:T(8,128)(2,1)} %k_hbm.1, bf16[1,128,768]{2,1,0:T(8,128)(2,1)} %v_hbm.1, s32[1,2048]{1,0:T(1,128)} %seg_hbm.1, f32[1]{0:T(128)S(6)} %copy.9.blend_ref, bf16[48,768]{1,0:T(8,128)(2,1)} %first_hbm.1, bf16[48,768]{1,0:T(8,128)(2,1)} %second_hbm.1), custom_call_target="tpu_custom_call" | custom-call | tf_op jit(solution)/shard_map/pallas_call | solution.py:403
  72.3 1.8 %copy.10 = bf16[1,128,1536]{2,1,0:T(8,128)(2,1)} copy(bf16[1,128,1536]{2,1,0:T(8,128)(2,1)} %shard_map.73) | data formatting | bytes 786432
